TPU v7x, 256 devices: a whole 4x4x8 slice. The times are simulated.
256 devices in a mesh: tok: 32 (over z, y_lo, core), tp: 8 (over y_hi, x).
Axes of the slice: x: 4, y: 4 (y_hi: 2, y_lo: 2; y = y_hi * 2 + y_lo), z: 8, core: 2. Of those that a mesh axis runs over, the one named last changes fastest.
Arguments:
- hidden_in: bfloat16 [8192, 4096], P('tok', 'tp'), may hold values from -6 to 6
- norm_gain: float32 [4096], replicated, may hold values from 0.5 to 9, as said below
- w_query: bfloat16 [4096, 4096], P(None, 'tp'), may hold values from -0.09375 to 0.09375
- w_key: bfloat16 [4096, 1024], P(None, 'tp'), may hold values from -0.09375 to 0.09375
- w_value: bfloat16 [4096, 1024], P(None, 'tp'), may hold values from -0.09375 to 0.09375
- w_out: bfloat16 [4096, 4096], P('tp'), may hold values from -0.5 to 0.5
- doc_ids: int32 [8192], replicated, may hold values from 0 to 3, never falling along the last dimension, each value on 1 to 6144 neighbouring positions
Outputs:
- hidden_out: bfloat16 [8192, 4096], P('tok', 'tp')
- joint_cov: float32 [2, 4096, 2, 4096], P(None, 'tok', None, 'tp')
Inputs may be any that keep to these rules, and one draw needn't show every extreme that they name: `norm_gain`: each channel's gain is positive. `doc_ids`: document numbers never fall along the tokens; a document holds 1 to 6144 tokens.
All inputs are finite; a program needn't handle non-finite values.
Results may differ from a plain program's by a relative error of at most 0.013.
The roundings to bfloat16 on the way count: a program that leaves them out, or rounds other values in their place, can miss the bound.
Values may be sent and summed in bfloat16 or wider, within the bound.
No kernel may reach another device: no remote copies, remote signals or barrier semaphores. Data moves between devices by JAX's collectives and lax.ppermute only.
A program may use at most 128 MiB of HBM per device.

v0:
```python
import jax
import jax.numpy as jnp
from jax import lax
from jax.sharding import PartitionSpec as P

HS = 128
epsilon = 1e-05
rope_base = 500000.0


def laid_out(blocks, dim):
    blocks = jnp.moveaxis(blocks, 0, dim)
    dims = blocks.shape
    return blocks.reshape(*dims[:dim], dims[dim] * dims[dim + 1], *dims[dim + 2 :])


def copy_for_each(x, axis):
    copies = jnp.broadcast_to(x, (lax.axis_size(axis), *x.shape))
    return lax.all_to_all(copies, axis, split_axis=0, concat_axis=0, tiled=True)


def collect(x, axis, dim):
    return laid_out(copy_for_each(x, axis), dim)


def in_one_piece(arrays, axis, dim, along):
    ends, at = ([], 0)
    for a in arrays[:-1]:
        at += a.shape[along]
        ends.append(at)
    both = jnp.concatenate(arrays, axis=along)
    return tuple(jnp.split(lax.all_gather(both, axis, axis=dim, tiled=True), ends, axis=along))


def rotate(vectors, positions):
    half_dim = vectors.shape[-1] // 2
    inv_freq = rope_base ** (-(jnp.arange(half_dim, dtype=jnp.float32) * 2.0) / vectors.shape[-1])
    angles = positions.astype(jnp.float32)[:, None] * inv_freq[None, :]
    cosine = jnp.cos(angles)[:, None, :]
    sine_part = jnp.sin(angles)[:, None, :]
    first_half = vectors[..., :half_dim]
    second_half = vectors[..., half_dim:]
    return jnp.concatenate(
        [
            first_half * cosine - second_half * sine_part,
            second_half * cosine + first_half * sine_part,
        ],
        axis=-1,
    )


def on_device(hidden_in, norm_gain, w_query, w_key, w_value, w_out, doc_ids):
    tok_rows = hidden_in.shape[0]
    col_width = hidden_in.shape[1]
    tok_count = lax.axis_size("tok")
    tok_index = lax.axis_index("tok")
    tp_index = lax.axis_index("tp")
    all_rows = tok_rows * tok_count
    full_in = collect(hidden_in, "tp", 1)
    model_width = full_in.shape[1]
    row_width = model_width // tok_count
    widened = full_in.astype(jnp.float32)
    factor = lax.rsqrt(jnp.mean(widened * widened, axis=1, keepdims=True) + epsilon)
    normed = (widened * factor * norm_gain[None, :]).astype(jnp.bfloat16)
    kv_heads = w_key.shape[1] // HS
    groups = w_query.shape[1] // w_key.shape[1]
    first_row = tok_index * tok_rows
    positions = first_row + jnp.arange(tok_rows, dtype=jnp.int32)
    key_local = rotate(
        jnp.dot(normed, w_key, preferred_element_type=jnp.float32).reshape(tok_rows, kv_heads, HS),
        positions % all_rows,
    )
    key_local = key_local.astype(jnp.bfloat16).reshape(tok_rows, kv_heads * HS)
    value_local = jnp.dot(normed, w_value, preferred_element_type=jnp.float32).astype(jnp.bfloat16)
    key_rows, value_rows = in_one_piece((key_local, value_local), "tok", 0, 1)
    queries = rotate(
        jnp.dot(normed, w_query, preferred_element_type=jnp.float32).reshape(
            tok_rows, kv_heads * groups, HS
        ),
        positions % all_rows,
    )
    queries = queries.astype(jnp.bfloat16).reshape(tok_rows, kv_heads, groups, HS)
    key_seq = key_rows.reshape(all_rows, kv_heads, HS)
    value_seq = value_rows.reshape(all_rows, kv_heads, HS)
    key_pos = jnp.arange(all_rows, dtype=jnp.int32)
    query_doc = lax.dynamic_slice_in_dim(doc_ids, first_row, tok_rows, 0)
    allowed = (query_doc[:, None] == doc_ids[None, :]) & (key_pos[None, :] <= positions[:, None])
    scores = jnp.einsum(
        "qhgd,khd->hgqk", queries, key_seq, preferred_element_type=jnp.float32
    ) * HS ** (-0.5)
    scores = jnp.where(allowed[None, None], scores, -jnp.inf)
    row_max = jnp.max(scores, axis=-1, keepdims=True)
    weights = jnp.exp(scores - row_max)
    weight_sum = jnp.sum(weights, axis=-1, keepdims=True)
    blended = (
        jnp.einsum(
            "hgqk,khd->hgqd",
            weights.astype(jnp.bfloat16),
            value_seq,
            preferred_element_type=jnp.float32,
        )
        / weight_sum
    )
    attended = (
        jnp.transpose(blended, (2, 0, 1, 3))
        .astype(jnp.bfloat16)
        .reshape(tok_rows, kv_heads * groups * HS)
    )
    partial_out = jnp.dot(attended, w_out, preferred_element_type=jnp.float32)
    summed = lax.psum(partial_out, "tp")
    full_out = (widened + summed).astype(jnp.bfloat16)
    hidden_out = lax.dynamic_slice_in_dim(full_out, tp_index * col_width, col_width, 1)
    joint_local = jnp.stack(
        [
            full_in.reshape(tok_rows, tok_count, row_width),
            full_out.reshape(tok_rows, tok_count, row_width),
        ],
        axis=1,
    )
    row_block = lax.all_to_all(joint_local, "tok", split_axis=2, concat_axis=0, tiled=True).reshape(
        all_rows, 2 * row_width
    )
    portion = lax.all_gather(jnp.stack([hidden_in, hidden_out], axis=1), "tok", axis=0, tiled=True)
    piece_rows = portion.shape[0]
    flat_part = portion.reshape(piece_rows, 2 * col_width)
    product = lax.dot_general(
        row_block, flat_part, (((0,), (0,)), ((), ())), preferred_element_type=jnp.float32
    )
    col_sum = jnp.sum(flat_part, axis=0, dtype=jnp.float32)
    row_mean = jnp.sum(row_block, axis=0, dtype=jnp.float32) / all_rows
    col_mean = col_sum / all_rows
    joint_cov = (product / all_rows - row_mean[:, None] * col_mean[None, :]).reshape(
        2, row_width, 2, col_width
    )
    return (hidden_out, joint_cov)


def solution(mesh):
    return jax.shard_map(
        on_device,
        mesh=mesh,
        in_specs=(
            P("tok", "tp"),
            P(),
            P(None, "tp"),
            P(None, "tp"),
            P(None, "tp"),
            P("tp", None),
            P(),
        ),
        out_specs=(P("tok", "tp"), P(None, "tok", None, "tp")),
        check_vma=False,
    )
```

profile of v0, /device:TPU:1, one launch (start us, length us, event | category | flops | bytes accessed | tf_op | source)
XLA Modules:
  0.0 543.1 jit_solution(12067020020564749845)
XLA Ops:
  7.2 1.2 copy.29
  8.4 1.5 broadcast_in_dim.10
  9.8 7.5 %all-to-all-start = ((bf16[8,256,512]{1,2,0:T(8,128)(2,1)}), bf16[8,256,512]{1,2,0:T(8,128)(2,1)S(1)}, u32[]{:S(2)}, u32[]{:S(2)}) async-start(bf16[8,256,512]{1,2,0:T(8,128)(2,1)} %broadcast_in_dim.10), calls=%async_computation | async-start | bytes 4194304 | tf_op jit(solution)/shard_map/all_to_all | solution.py:19
  17.4 28.5 %all-to-all-done = bf16[8,256,512]{1,2,0:T(8,128)(2,1)S(1)} async-done(((bf16[8,256,512]{1,2,0:T(8,128)(2,1)}), bf16[8,256,512]{1,2,0:T(8,128)(2,1)S(1)}, u32[]{:S(2)}, u32[]{:S(2)}) %all-to-all-start) | async-done | bytes 2097184 | tf_op jit(solution)/shard_map/all_to_all | solution.py:19
  46.5 2.3 bitcast_convert_fusion
  48.8 5.7 %copy.44 = f32[256,4096]{1,0:T(8,128)} copy(f32[256,4096]{0,1:T(8,128)} %bitcast.92) | data formatting | bytes 8388608 | tf_op jit(solution)/shard_map/convert_element_type | solution.py:62
  54.4 2.9 multiply_convert_fusion.1
  60.3 6.4 %copy.47 = bf16[512,4096]{1,0:T(8,128)(2,1)} copy(bf16[512,4096]{0,1:T(8,128)(2,1)} %bitcast.95) | data formatting | bytes 8388608 | tf_op jit(solution)/shard_map/dot_general | solution.py:77
  67.1 4.7 fusion.7
  72.5 1.3 fusion.34
  73.8 61.0 %all-gather.3.cloned.1.call-done = bf16[8192,256]{0,1:T(8,128)(2,1)} async-done(((bf16[256,256]{0,1:T(8,128)(2,1)}), bf16[8192,256]{0,1:T(8,128)(2,1)}) %all-gather.3.cloned.1.call-update) | async-done | bytes 4194320 | tf_op jit(solution)/shard_map/all_gather | solution.py:32
  134.9 15.3 %fusion.2 = (f32[4,256]{1,0:T(4,128)S(1)}, f32[8192,256,4]{1,0,2:T(8,128)}) fusion(pred[256,8192]{0,1:T(8,128)(4,1)} %fusion.7, bf16[256,4,64]{0,2,1:T(8,128)(2,1)S(1)} %get-tuple-element.3, bf16[256,4,64]{0,2,1:T(8,128)(2,1)S(1)} %get-tuple-element.2, bf16[8192,256]{0,1:T(8,128)(2,1)} %all-gather.3.cloned.1.call-done), kind=kOutput, calls=%fused_computation.5 | convolution fusion | flops 2173172736 | bytes 38014976 | tf_op jit(solution)/shard_map/qhgd,khd->hgqk/dot_general | solution.py:88
  150.2 14.5 %fusion = f32[4,256]{1,0:T(4,128)S(1)} fusion(f32[8192,256,4]{1,0,2:T(8,128)} %get-tuple-element.9, f32[4,256]{1,0:T(4,128)S(1)} %get-tuple-element.8, pred[256,8192]{0,1:T(8,128)(4,1)S(1)} %copy-done.3), kind=kLoop, calls=%fused_computation.3 | loop fusion | flops 33553408 | bytes 35659776 | tf_op jit(solution)/shard_map/reduce_sum | solution.py:94
  164.7 15.5 %fusion.13 = bf16[4,256,128]{1,2,0:T(8,128)(2,1)S(1)} fusion(f32[8192,256,4]{1,0,2:T(8,128)} %get-tuple-element.9, f32[4,256]{1,0:T(4,128)S(1)} %get-tuple-element.8, pred[256,8192]{0,1:T(8,128)(4,1)} %fusion.7, bf16[8192,256]{0,1:T(8,128)(2,1)} %all-gather.3.cloned.1.call-done, f32[4,256]{1,0:T(4,128)S(1)} %fusion), kind=kOutput, calls=%fused_computation.26 | convolution fusion | flops 2181300224 | bytes 38019072 | tf_op jit(solution)/shard_map/hgqk,khd->hgqd/dot_general | solution.py:96
  180.2 5.5 %fusion.35 = f32[256,4096]{1,0:T(8,128)} fusion(bf16[256,512]{0,1:T(8,128)(2,1)S(1)} %bitcast.100, bf16[512,4096]{1,0:T(8,128)(2,1)} %param.12), kind=kOutput, calls=%fused_computation.63 | convolution fusion | flops 1073741824 | bytes 8650752 | tf_op jit(solution)/shard_map/dot_general | solution.py:109
  185.7 113.2 %all-reduce.2.cloned.1.call-done = f32[256,4096]{1,0:T(8,128)} async-done(((f32[256,4096]{1,0:T(8,128)}), f32[256,4096]{1,0:T(8,128)}) %all-reduce.2.cloned.1.call-update) | async-done | bytes 4194320 | tf_op jit(solution)/shard_map/psum | solution.py:110
  298.9 4.0 add_convert_fusion
  302.9 1.4 copy-done.2
  305.1 4.1 copy.48
  309.2 2.0 pad_maximum_fusion
  311.2 2.3 copy.37
  313.5 7.9 %all-to-all-start.1 = ((bf16[256,2,32,128]{0,3,1,2:T(8,128)(2,1)}), bf16[256,2,32,128]{0,3,1,2:T(8,128)(2,1)}, u32[]{:S(2)}, u32[]{:S(2)}) async-start(bf16[256,2,32,128]{0,3,1,2:T(8,128)(2,1)} %copy.37), calls=%async_computation.1 | async-start | bytes 8388608 | tf_op jit(solution)/shard_map/all_to_all | solution.py:120
  321.4 1.7 constant_dynamic-slice_fusion
  323.1 139.7 %all-to-all-done.1 = bf16[256,2,32,128]{0,3,1,2:T(8,128)(2,1)} async-done(((bf16[256,2,32,128]{0,3,1,2:T(8,128)(2,1)}), bf16[256,2,32,128]{0,3,1,2:T(8,128)(2,1)}, u32[]{:S(2)}, u32[]{:S(2)}) %all-to-all-start.1) | async-done | bytes 4194336 | tf_op jit(solution)/shard_map/all_to_all | solution.py:120
  462.8 4.6 copy.38
  467.4 6.4 %copy.49 = bf16[32,8,32,256]{3,1,2,0:T(8,128)(2,1)} copy(bf16[32,8,32,256]{3,2,1,0:T(8,128)(2,1)S(1)} %bitcast.93) | data formatting | bytes 8388608
  473.8 2.9 convert_reduce_fusion.1
  476.7 17.3 %all-gather.5.cloned.1.call-done = bf16[8192,2,512]{2,0,1:T(8,128)(2,1)} async-done(((bf16[256,2,512]{2,0,1:T(8,128)(2,1)}), bf16[8192,2,512]{2,0,1:T(8,128)(2,1)}) %all-gather.5.cloned.1.call-update) | async-done | bytes 16777232 | tf_op jit(solution)/shard_map/all_gather | solution.py:123
  494.0 10.3 %convert_reduce_fusion = f32[2,512]{1,0:T(2,128)S(1)} fusion(bf16[8192,2,512]{2,0,1:T(8,128)(2,1)} %all-gather.5.cloned.1.call-done), kind=kLoop, calls=%fused_computation.1 | loop fusion | flops 16776192 | bytes 16781312 | tf_op jit(solution)/shard_map/reduce_sum | solution.py:129
  504.4 20.9 %copy.39 = bf16[8192,2,512]{0,2,1:T(8,128)(2,1)} copy(bf16[8192,2,512]{2,0,1:T(8,128)(2,1)} %all-gather.5.cloned.1.call-done) | data formatting | bytes 33554432 | tf_op jit(solution)/shard_map/all_gather | solution.py:123
  525.3 9.4 %fusion.9 = f32[256,1024]{1,0:T(8,128)S(1)} fusion(bf16[8192,256]{0,1:T(8,128)(2,1)} %bitcast.97, bf16[8192,1024]{0,1:T(8,128)(2,1)} %bitcast.91, f32[1024]{0:T(1024)S(1)} %bitcast.101, f32[256]{0:T(256)S(1)} %multiply_bitcast_fusion.1), kind=kOutput, calls=%fused_computation.22 | convolution fusion | flops 4295753728 | bytes 22025216 | tf_op jit(solution)/shard_map/dot_general | solution.py:126
  534.7 1.9 reshape.283
  (42 shorter events, 5.7 us)
Async XLA Ops:
  7.2 50.1 %copy-start = (bf16[4096,128]{1,0:T(8,128)(2,1)S(1)}, bf16[4096,128]{1,0:T(8,128)(2,1)}, u32[]{:S(2)}) copy-start(bf16[4096,128]{1,0:T(8,128)(2,1)} %param.11) | copy-start | bytes 3145732
  9.8 36.0 %all-to-all-start = ((bf16[8,256,512]{1,2,0:T(8,128)(2,1)}), bf16[8,256,512]{1,2,0:T(8,128)(2,1)S(1)}, u32[]{:S(2)}, u32[]{:S(2)}) async-start(bf16[8,256,512]{1,2,0:T(8,128)(2,1)} %broadcast_in_dim.10), calls=%async_computation | async-start | bytes 4194304 | tf_op jit(solution)/shard_map/all_to_all | solution.py:19
  17.3 117.6 %all-gather.3.cloned.1.call-start = ((), (), s32[]{:S(2)}) async-start(), calls=%async_computation.2 | async-start | bytes 4325376 | tf_op jit(solution)/shard_map/all_gather | solution.py:32
  48.8 5.7 %copy-start.7 = (f32[4096]{0:T(1024)S(1)}, f32[4096]{0:T(1024)}, u32[]{:S(2)}) copy-start(f32[4096]{0:T(1024)} %param.8) | copy-start | bytes 49156
  54.4 3.7 copy-start.5
  60.0 238.9 %all-reduce.2.cloned.1.call-start = ((), (), s32[]{:S(2)}) async-start(), calls=%async_computation.3 | async-start | bytes 8388608 | tf_op jit(solution)/shard_map/psum | solution.py:110
  60.2 6.5 %copy-start.8 = (s32[8192]{0:T(1024)S(1)}, s32[8192]{0:T(1024)}, u32[]{:S(2)}) copy-start(s32[8192]{0:T(1024)} %param.13) | copy-start | bytes 98308
  66.7 5.8 %copy-start.4 = (bf16[512,4096]{1,0:T(8,128)(2,1)S(1)}, bf16[512,4096]{1,0:T(8,128)(2,1)}, u32[]{:S(2)}) copy-start(bf16[512,4096]{1,0:T(8,128)(2,1)} %copy.47) | copy-start | bytes 12582916
  134.9 15.3 %copy-start.3 = (pred[256,8192]{0,1:T(8,128)(4,1)S(1)}, pred[256,8192]{0,1:T(8,128)(4,1)}, u32[]{:S(2)}) copy-start(pred[256,8192]{0,1:T(8,128)(4,1)} %fusion.7) | copy-start | bytes 6291460
  185.6 308.4 %all-gather.5.cloned.1.call-start = ((), (), s32[]{:S(2)}) async-start(), calls=%async_computation.4 | async-start | bytes 17301504 | tf_op jit(solution)/shard_map/all_gather | solution.py:123
  185.7 118.6 %copy-start.6 = (bf16[256,512]{1,0:T(8,128)(2,1)S(1)}, bf16[256,512]{1,0:T(8,128)(2,1)}, u32[]{:S(2)}) copy-start(bf16[256,512]{1,0:T(8,128)(2,1)} %param.7) | copy-start | bytes 786436
  302.9 1.4 copy-start.2
  313.5 149.3 %all-to-all-start.1 = ((bf16[256,2,32,128]{0,3,1,2:T(8,128)(2,1)}), bf16[256,2,32,128]{0,3,1,2:T(8,128)(2,1)}, u32[]{:S(2)}, u32[]{:S(2)}) async-start(bf16[256,2,32,128]{0,3,1,2:T(8,128)(2,1)} %copy.37), calls=%async_computation.1 | async-start | bytes 8388608 | tf_op jit(solution)/shard_map/all_to_all | solution.py:120
  525.3 11.3 %copy-start.1 = (bf16[4096,128]{1,0:T(8,128)(2,1)S(1)}, bf16[4096,128]{1,0:T(8,128)(2,1)}, u32[]{:S(2)}) copy-start(bf16[4096,128]{1,0:T(8,128)(2,1)} %param.11) | copy-start | bytes 3145732
Sparse Core Ops, SparseCore 0:
  60.1 74.7 all-gather.2
  185.8 113.0 all-reduce.1
  305.3 188.7 all-gather.4
where the time goes:
time: 544 us; the launch traced here: 543 us
  waiting for transfers between devices  360 us (66%)
  local copies, waits for them, and re-layouts  58 us (11%)
  matrix products  48.6 us (9%)
  other arithmetic  47.1 us (9%)
  starting transfers between devices  15.7 us (3%)
  between operations  14 us (3%)
    all_to_all x1, waiting for transfers between devices, on_device(): lax.all_to_all(joint_local, 'tok', split_axis=2, concat_axis=0, tiled=True)  140 us
    psum x1, waiting for transfers between devices, on_device(): summed = lax.psum(partial_out, 'tp')  113 us
    all_gather x1, waiting for transfers between devices, in_one_piece(): lax.all_gather(both, axis, axis=dim, tiled=True)  61 us
    all_to_all x1, waiting for transfers between devices, copy_for_each(): return lax.all_to_all(copies, axis, split_axis=0, concat_axis=0, tiled=True)  28.5 us
    all_gather x1, local copies, waits for them, and re-layouts, on_device(): lax.all_gather(jnp.stack([hidden_in, hidden_out], axis=1), 'tok', axis=0,...  20.9 us
    all_gather x1, waiting for transfers between devices, on_device(): lax.all_gather(jnp.stack([hidden_in, hidden_out], axis=1), 'tok', axis=0,...  17.3 us
    dot_general x1, matrix products, on_device(): jnp.einsum('hgqk,khd->hgqd', weights.astype(jnp.bfloat16), value_seq, pre...  15.5 us
    dot_general x1, matrix products, on_device(): jnp.einsum('qhgd,khd->hgqk', queries, key_seq, preferred_element_type=jnp...  15.3 us
  transfers between devices with their start and end apart: 5, of which 5 were waited for; matrix products, arithmetic and copies ran while one was open for 7% of the time, Pallas kernels for 0%

commit v1 on v0

--- a/solution.py
+++ b/solution.py
@@ -120,7 +120,15 @@
     row_block = lax.all_to_all(joint_local, "tok", split_axis=2, concat_axis=0, tiled=True).reshape(
         all_rows, 2 * row_width
     )
-    portion = lax.all_gather(jnp.stack([hidden_in, hidden_out], axis=1), "tok", axis=0, tiled=True)
+    portion = jnp.concatenate(
+        lax.all_to_all(
+            jnp.stack(lax.axis_size("tok") * [jnp.stack([hidden_in, hidden_out], axis=1)]),
+            axis_name="tok",
+            split_axis=0,
+            concat_axis=0,
+        ),
+        axis=0,
+    )
     piece_rows = portion.shape[0]
     flat_part = portion.reshape(piece_rows, 2 * col_width)
     product = lax.dot_general(

time: 544 us -> 850 us (1.56)
  waiting for transfers between devices: 360 us -> 646 us
  local copies, waits for them, and re-layouts: 58 us -> 72 us
    all_to_all x0 -> x1, waiting for transfers between devices: none -> 351 us  [on_device(): lax.all_to_all(jnp.stack(lax.axis_size('tok') * [jnp.stack([hidden_in, hi...]
    all_to_all x1, waiting for transfers between devices: 140 us -> 92.8 us  [on_device(): lax.all_to_all(joint_local, 'tok', split_axis=2, concat_axis=0, tiled=True)]
    all_gather x1 -> x0, local copies, waits for them, and re-layouts: 20.9 us -> none  [on_device(): lax.all_gather(jnp.stack([hidden_in, hidden_out], axis=1), 'tok', axis=0,...]
    all_gather x1 -> x0, waiting for transfers between devices: 17.3 us -> none  [on_device(): lax.all_gather(jnp.stack([hidden_in, hidden_out], axis=1), 'tok', axis=0,...]
    all_to_all x0 -> x1, local copies, waits for them, and re-layouts: none -> 15.5 us  [on_device(): lax.all_to_all(jnp.stack(lax.axis_size('tok') * [jnp.stack([hidden_in, hi...]
    unnamed x21 -> x20, local copies, waits for them, and re-layouts: 8.93 us -> 21.3 us
  transfers between devices with their start and end apart: 5 -> 5, of which waited for: 5 -> 5; matrix products, arithmetic and copies ran while one was open for 7% -> 4% of each run, Pallas kernels for 0% -> 0%
where the time goes in v1:
time: 850 us; the launch traced here: 849 us
  waiting for transfers between devices  646 us (76%)
  local copies, waits for them, and re-layouts  72 us (8%)
  matrix products  48.8 us (6%)
  other arithmetic  44.1 us (5%)
  starting transfers between devices  23.5 us (3%)
  between operations  14.3 us (2%)
    all_to_all x1, waiting for transfers between devices, on_device(): lax.all_to_all(jnp.stack(lax.axis_size('tok') * [jnp.stack([hidden_in, hi...  351 us
    psum x1, waiting for transfers between devices, on_device(): summed = lax.psum(partial_out, 'tp')  113 us
    all_to_all x1, waiting for transfers between devices, on_device(): lax.all_to_all(joint_local, 'tok', split_axis=2, concat_axis=0, tiled=True)  92.8 us
    all_gather x1, waiting for transfers between devices, in_one_piece(): lax.all_gather(both, axis, axis=dim, tiled=True)  61 us
    all_to_all x1, waiting for transfers between devices, copy_for_each(): return lax.all_to_all(copies, axis, split_axis=0, concat_axis=0, tiled=True)  28.5 us
    unnamed x20, local copies, waits for them, and re-layouts  21.3 us
  transfers between devices with their start and end apart: 5, of which 5 were waited for; matrix products, arithmetic and copies ran while one was open for 4% of the time, Pallas kernels for 0%

profile of v1, /device:TPU:1, one launch (start us, length us, event | category | flops | bytes accessed | tf_op | source)
XLA Modules:
  0.0 849.1 jit_solution(3518026693929016349)
XLA Ops:
  8.4 1.5 broadcast_in_dim.10
  9.8 7.5 all-to-all-start
  17.4 28.5 %all-to-all-done = bf16[8,256,512]{1,2,0:T(8,128)(2,1)S(1)} async-done(((bf16[8,256,512]{1,2,0:T(8,128)(2,1)}), bf16[8,256,512]{1,2,0:T(8,128)(2,1)S(1)}, u32[]{:S(2)}, u32[]{:S(2)}) %all-to-all-start) | async-done | bytes 2097184 | tf_op jit(solution)/shard_map/all_to_all | solution.py:19
  46.5 2.3 bitcast_convert_fusion
  48.8 5.7 copy.80
  54.5 2.9 multiply_convert_fusion.1
  60.3 6.4 copy.83
  67.2 4.7 fusion.7
  73.9 61.0 %all-gather.2.cloned.1.call-done = bf16[8192,256]{0,1:T(8,128)(2,1)} async-done(((bf16[256,256]{0,1:T(8,128)(2,1)}), bf16[8192,256]{0,1:T(8,128)(2,1)}) %all-gather.2.cloned.1.call-update) | async-done | bytes 4194320 | tf_op jit(solution)/shard_map/all_gather | solution.py:32
  135.0 15.3 %fusion.2 = (f32[4,256]{1,0:T(4,128)S(1)}, f32[8192,256,4]{1,0,2:T(8,128)}) fusion(pred[256,8192]{0,1:T(8,128)(4,1)} %fusion.7, bf16[256,4,64]{0,2,1:T(8,128)(2,1)S(1)} %get-tuple-element.3, bf16[256,4,64]{0,2,1:T(8,128)(2,1)S(1)} %get-tuple-element.2, bf16[8192,256]{0,1:T(8,128)(2,1)} %all-gather.2.cloned.1.call-done), kind=kOutput, calls=%fused_computation.5 | convolution fusion | flops 2173172736 | bytes 38014976 | tf_op jit(solution)/shard_map/qhgd,khd->hgqk/dot_general | solution.py:88
  150.3 14.5 %fusion = f32[4,256]{1,0:T(4,128)S(1)} fusion(f32[8192,256,4]{1,0,2:T(8,128)} %get-tuple-element.9, f32[4,256]{1,0:T(4,128)S(1)} %get-tuple-element.8, pred[256,8192]{0,1:T(8,128)(4,1)S(1)} %copy-done.2), kind=kLoop, calls=%fused_computation.3 | loop fusion | flops 33553408 | bytes 35659776 | tf_op jit(solution)/shard_map/reduce_sum | solution.py:94
  164.8 15.5 %fusion.13 = bf16[4,256,128]{1,2,0:T(8,128)(2,1)S(1)} fusion(f32[8192,256,4]{1,0,2:T(8,128)} %get-tuple-element.9, f32[4,256]{1,0:T(4,128)S(1)} %get-tuple-element.8, pred[256,8192]{0,1:T(8,128)(4,1)} %fusion.7, bf16[8192,256]{0,1:T(8,128)(2,1)} %all-gather.2.cloned.1.call-done, f32[4,256]{1,0:T(4,128)S(1)} %fusion), kind=kOutput, calls=%fused_computation.26 | convolution fusion | flops 2181300224 | bytes 38019072 | tf_op jit(solution)/shard_map/hgqk,khd->hgqd/dot_general | solution.py:96
  180.2 5.4 fusion.35
  185.7 113.3 %all-reduce.2.cloned.1.call-done = f32[256,4096]{1,0:T(8,128)} async-done(((f32[256,4096]{1,0:T(8,128)}), f32[256,4096]{1,0:T(8,128)}) %all-reduce.2.cloned.1.call-update) | async-done | bytes 4194320 | tf_op jit(solution)/shard_map/psum | solution.py:110
  299.0 5.3 add_convert_fusion
  304.3 4.1 copy.84
  308.4 2.0 pad_maximum_fusion
  310.4 2.2 copy.71
  312.6 8.0 all-to-all-start.1
  321.9 92.8 %all-to-all-done.1 = bf16[256,2,32,128]{0,3,1,2:T(8,128)(2,1)} async-done(((bf16[256,2,32,128]{0,3,1,2:T(8,128)(2,1)}), bf16[256,2,32,128]{0,3,1,2:T(8,128)(2,1)}, u32[]{:S(2)}, u32[]{:S(2)}) %all-to-all-start.1) | async-done | bytes 4194336 | tf_op jit(solution)/shard_map/all_to_all | solution.py:120
  414.7 5.9 stack.14
  420.6 7.7 all-to-all-start.2
  428.3 1.7 constant_dynamic-slice_fusion
  430.0 4.6 copy.72
  434.6 6.2 copy.86
  440.8 2.9 convert_reduce_fusion.1
  443.7 350.8 %all-to-all-done.2 = bf16[32,256,2,512]{1,3,2,0:T(8,128)(2,1)} async-done(((bf16[32,256,2,512]{1,3,2,0:T(8,128)(2,1)}), bf16[32,256,2,512]{1,3,2,0:T(8,128)(2,1)}, u32[]{:S(2)}, u32[]{:S(2)}) %all-to-all-start.2) | async-done | bytes 16777248 | tf_op jit(solution)/shard_map/all_to_all | solution.py:124
  794.5 15.5 %copy.74 = bf16[32,256,2,512]{1,0,3,2:T(8,128)(2,1)S(1)} copy(bf16[32,256,2,512]{1,3,2,0:T(8,128)(2,1)} %all-to-all-done.2) | data formatting | bytes 33554432 | tf_op jit(solution)/shard_map/all_to_all | solution.py:124
  810.0 13.8 %copy.87 = bf16[128,8,32,256]{3,1,2,0:T(8,128)(2,1)} copy(bf16[128,8,32,256]{3,2,1,0:T(8,128)(2,1)S(1)} %bitcast.94) | data formatting | bytes 33554432
  823.8 6.9 convert_reduce_fusion
  830.7 9.7 %fusion.9 = f32[256,1024]{1,0:T(8,128)S(1)} fusion(bf16[8192,256]{0,1:T(8,128)(2,1)} %bitcast.101, bf16[8192,1024]{0,1:T(8,128)(2,1)} %bitcast.96, f32[1024]{0:T(1024)S(1)} %bitcast.106, f32[256]{0:T(256)S(1)} %multiply_bitcast_fusion.1), kind=kOutput, calls=%fused_computation.22 | convolution fusion | flops 4295753728 | bytes 22025216 | tf_op jit(solution)/shard_map/dot_general | solution.py:134
  840.4 1.9 reshape.281
  (42 shorter events, 8.4 us)
Async XLA Ops:
  7.2 50.2 %copy-start = (bf16[4096,128]{1,0:T(8,128)(2,1)S(1)}, bf16[4096,128]{1,0:T(8,128)(2,1)}, u32[]{:S(2)}) copy-start(bf16[4096,128]{1,0:T(8,128)(2,1)} %param.11) | copy-start | bytes 3145732
  9.8 36.0 %all-to-all-start = ((bf16[8,256,512]{1,2,0:T(8,128)(2,1)}), bf16[8,256,512]{1,2,0:T(8,128)(2,1)S(1)}, u32[]{:S(2)}, u32[]{:S(2)}) async-start(bf16[8,256,512]{1,2,0:T(8,128)(2,1)} %broadcast_in_dim.10), calls=%async_computation | async-start | bytes 4194304 | tf_op jit(solution)/shard_map/all_to_all | solution.py:19
  17.3 117.6 %all-gather.2.cloned.1.call-start = ((), (), s32[]{:S(2)}) async-start(), calls=%async_computation.3 | async-start | bytes 4325376 | tf_op jit(solution)/shard_map/all_gather | solution.py:32
  48.8 5.7 copy-start.6
  54.5 3.7 copy-start.4
  60.1 238.9 %all-reduce.2.cloned.1.call-start = ((), (), s32[]{:S(2)}) async-start(), calls=%async_computation.4 | async-start | bytes 8388608 | tf_op jit(solution)/shard_map/psum | solution.py:110
  60.3 6.5 copy-start.7
  66.8 5.8 copy-start.3
  135.0 15.3 %copy-start.2 = (pred[256,8192]{0,1:T(8,128)(4,1)S(1)}, pred[256,8192]{0,1:T(8,128)(4,1)}, u32[]{:S(2)}) copy-start(pred[256,8192]{0,1:T(8,128)(4,1)} %fusion.7) | copy-start | bytes 6291460
  312.6 9.0 %copy-start.5 = (bf16[256,512]{1,0:T(8,128)(2,1)S(1)}, bf16[256,512]{1,0:T(8,128)(2,1)}, u32[]{:S(2)}) copy-start(bf16[256,512]{1,0:T(8,128)(2,1)} %param.7) | copy-start | bytes 786436
  312.6 102.1 %all-to-all-start.1 = ((bf16[256,2,32,128]{0,3,1,2:T(8,128)(2,1)}), bf16[256,2,32,128]{0,3,1,2:T(8,128)(2,1)}, u32[]{:S(2)}, u32[]{:S(2)}) async-start(bf16[256,2,32,128]{0,3,1,2:T(8,128)(2,1)} %copy.71), calls=%async_computation.1 | async-start | bytes 8388608 | tf_op jit(solution)/shard_map/all_to_all | solution.py:120
  420.6 373.9 %all-to-all-start.2 = ((bf16[32,256,2,512]{1,3,2,0:T(8,128)(2,1)}), bf16[32,256,2,512]{1,3,2,0:T(8,128)(2,1)}, u32[]{:S(2)}, u32[]{:S(2)}) async-start(bf16[32,256,2,512]{1,3,2,0:T(8,128)(2,1)} %stack.14), calls=%async_computation.2 | async-start | bytes 33554432 | tf_op jit(solution)/shard_map/all_to_all | solution.py:124
  830.7 11.5 %copy-start.1 = (bf16[4096,128]{1,0:T(8,128)(2,1)S(1)}, bf16[4096,128]{1,0:T(8,128)(2,1)}, u32[]{:S(2)}) copy-start(bf16[4096,128]{1,0:T(8,128)(2,1)} %param.11) | copy-start | bytes 3145732
Sparse Core Ops, SparseCore 0:
  60.2 74.7 all-gather.1
  185.8 113.1 all-reduce.1
